TPU v7x, 128 devices: a whole 4x4x4 slice. The times are simulated.
128 devices in a mesh: gz: 8 (over y, core), xy: 16 (over z, x).
Axes of the slice: x: 4, y: 4, z: 4, core: 2. Of those that a mesh axis runs over, the one named last changes fastest.
Arguments:
- velocity: float32 [128, 512, 1024], P('gz', 'xy'), may hold values from -6 to 6
- yield_stress: float32 [128, 512, 1024], P('gz', 'xy'), may hold values from 0.2 to 2
- stress_step: float32 [128, 512, 1024], P('gz', 'xy'), may hold values from -6 to 6
- block_weights: bfloat16 [8192, 32, 128], P(('gz', 'xy')), may hold values from -0.5 to 0.5
- block_cells: int32 [8192, 128], P(('gz', 'xy')), may hold values from 0 to 524287
- block_plane: int32 [8192], P(('gz', 'xy')), may hold values from 0 to 40
Outputs:
- stress_product: float32 [128, 512, 1024], P('gz', 'xy')
- plane_obs: float32 [40, 32], replicated
Inputs may be any that keep to these rules, and one draw needn't show every extreme that they name: `block_plane`: value 40 marks an empty slot. `block_cells`: flat index into the brick of the device that holds the block; cells may repeat.
All inputs are finite; a program needn't handle non-finite values.
Results may differ from a plain program's by a relative error of at most 0.0003.
Values sent between devices are 32-bit elements; how exact they have to be, the bound alone decides.
A program may use at most 192 MiB of HBM per device.

v0:
```python
import functools
import jax
import jax.numpy as jnp
from jax import lax
from jax.experimental import pallas as pl
from jax.experimental.pallas import tpu as pltpu
from jax.sharding import PartitionSpec as P

PLANES = 40
KEEP = 0.2
DAMP = 0.8
MESH = pl.DeviceIdType.MESH
F32 = jnp.float32
BF16 = jnp.bfloat16
VMEM = pl.BlockSpec(memory_space=pltpu.VMEM)
SMEM = pl.BlockSpec(memory_space=pltpu.SMEM)
ANY = pl.BlockSpec(memory_space=pl.ANY)
LIMIT = 56 * 1024 * 1024


def ids(shape):
    rank = len(shape)
    return (
        lax.broadcasted_iota(jnp.int32, shape, rank - 2),
        lax.broadcasted_iota(jnp.int32, shape, rank - 1),
    )


def x_next(a, wrap=True):
    sub, lane = ids(a.shape)
    r = pltpu.roll(a, 127, a.ndim - 1)
    r = jnp.where(lane == 127, pltpu.roll(r, 7, a.ndim - 2), r)
    return r if wrap else jnp.where((lane == 127) & (sub == 7), 0.0, r)


def x_prev(a, wrap=True):
    sub, lane = ids(a.shape)
    r = pltpu.roll(a, 1, a.ndim - 1)
    r = jnp.where(lane == 0, pltpu.roll(r, 1, a.ndim - 2), r)
    return r if wrap else jnp.where((lane == 0) & (sub == 0), 0.0, r)


def divisor(n, most):
    return max(d for d in range(1, most + 1) if n % d == 0)


class Faces:
    def __init__(self, CZ, CY, send, recv):
        self.CZ, self.CY, self.send, self.recv = CZ, CY, send, recv
        G, X = lax.axis_size("gz"), lax.axis_size("xy")
        g, x = lax.axis_index("gz"), lax.axis_index("xy")
        self.has = (g > 0, g < G - 1, x > 0, x < X - 1)
        lower, upper = jnp.maximum(g - 1, 0), jnp.minimum(g + 1, G - 1)
        left, right = jnp.maximum(x - 1, 0), jnp.minimum(x + 1, X - 1)
        self.to = ((lower, x), (upper, x), (g, left), (g, right))

    def copy(self, buf, e, d):
        CZ, CY = self.CZ, self.CY
        zs, ys = pl.ds(1, CZ), pl.ds(1, CY)
        src = (buf.at[1, ys], buf.at[CZ, ys], buf.at[zs, 1], buf.at[zs, CY])[d]
        dst = (buf.at[CZ + 1, ys], buf.at[0, ys], buf.at[zs, CY + 1], buf.at[zs, 0])[d]
        return pltpu.make_async_remote_copy(
            src_ref=src,
            dst_ref=dst,
            send_sem=self.send.at[e, d],
            recv_sem=self.recv.at[e, d],
            device_id=self.to[d],
            device_id_type=MESH,
        )

    def start(self, buf, e, which=(0, 1, 2, 3)):
        for d in which:

            @pl.when(self.has[d])
            def _():
                self.copy(buf, e, d).start()

    def arrive(self, buf, e):
        for d in range(4):

            @pl.when(self.has[d ^ 1])
            def _():
                self.copy(buf, e, d).wait_recv()

    def finish(self, buf, e):
        for d in range(4):

            @pl.when(self.has[d])
            def _():
                self.copy(buf, e, d).wait_send()


def lines():
    G, X = lax.axis_size("gz"), lax.axis_size("xy")
    g, x = lax.axis_index("gz"), lax.axis_index("xy")
    across = min(X, 4)
    return (
        (2, g % 2, lambda t: ((g // 2) * 2 + t, x)),
        (G // 2, g // 2, lambda t: (t * 2 + g % 2, x)),
        (across, x % across, lambda t: (g, (x // across) * across + t)),
        (X // across, x // across, lambda t: (g, t * across + x % across)),
    )


def greet(all_lines):
    G, X = lax.axis_size("gz"), lax.axis_size("xy")
    g, x = lax.axis_index("gz"), lax.axis_index("xy")
    sem = pltpu.get_barrier_semaphore()
    count = jnp.int32(0)
    for has, to in (
        (g > 0, (jnp.maximum(g - 1, 0), x)),
        (g < G - 1, (jnp.minimum(g + 1, G - 1), x)),
        (x > 0, (g, jnp.maximum(x - 1, 0))),
        (x < X - 1, (g, jnp.minimum(x + 1, X - 1))),
    ):
        count = count + has.astype(jnp.int32)

        @pl.when(has)
        def _():
            pl.semaphore_signal(sem, inc=1, device_id=to, device_id_type=MESH)

    if all_lines:
        for n, me, target in lines():
            for d in range(1, n):
                to = target(lax.rem(me + d, n))
                pl.semaphore_signal(sem, inc=1, device_id=to, device_id_type=MESH)
            count = count + (n - 1)
    pl.semaphore_wait(sem, count)


def clear_faces(bufs, CZ, CY):
    plane = jnp.zeros((CY + 2, 8, 128), F32)
    row = jnp.zeros((CZ, 8, 128), F32)
    for buf in bufs:
        buf[0] = plane
        buf[CZ + 1] = plane
        buf[pl.ds(1, CZ), 0] = row
        buf[pl.ds(1, CZ), CY + 1] = row


def interior(CZ, CY, f, planes):
    yn = divisor(CY - 2, 6)
    planes = divisor(CZ - 2, planes)

    @pl.loop(0, (CZ - 2) // planes)
    def _(i):
        for p in range(planes):
            for y in range(1, CY - 1, yn):
                f(1 + i * planes + p, y, 1, yn)


def boundary_z(CZ, CY, f):
    yn = divisor(CY, 8)

    @pl.loop(0, 2)
    def _(i):
        for y in range(0, CY, yn):
            f(i * (CZ - 1), y, 1, yn)


def boundary_y(CZ, CY, f):
    zn = divisor(CZ - 2, 8)
    for y in (0, CY - 1):
        for z in range(1, CZ - 1, zn):
            f(z, y, zn, 1)


def around(ref, z, y, zn, yn):
    zs, ys = pl.ds(z + 1, zn), pl.ds(y + 1, yn)
    if zn == 1:
        wide = ref[zs, pl.ds(y, yn + 2)]
        return (
            wide[:, 1 : yn + 1],
            wide[:, :yn],
            wide[:, 2:],
            ref[pl.ds(z, 1), ys],
            ref[pl.ds(z + 2, 1), ys],
        )
    wide = ref[pl.ds(z, zn + 2), ys]
    return (
        wide[1 : zn + 1],
        ref[zs, pl.ds(y, yn)],
        ref[zs, pl.ds(y + 2, yn)],
        wide[:zn],
        wide[2:],
    )


def coefficients(MU, z, y, zn, yn):
    m, ym, yp, zm, zp = around(MU, z, y, zn, yn)
    xm, xp = x_prev(m, False), x_next(m, False)
    total = ((xm + xp) + (ym + yp)) + (zm + zp)
    dinv = DAMP / (1.0 + (3.0 * m + 0.5 * total))
    half = 0.5 * dinv
    sub, lane = ids(m.shape)
    first, last = (sub == 0) & (lane == 0), (sub == 7) & (lane == 127)
    faces = (
        jnp.where(first, 0.0, half * (m + xm)),
        jnp.where(last, 0.0, half * (m + xp)),
        half * (m + ym),
        half * (m + yp),
        half * (m + zm),
        half * (m + zp),
    )
    return faces, dinv


def sweep(A, R, src, put, z, y, zn, yn):
    w, ym, yp, zm, zp = around(src, z, y, zn, yn)
    zs, ys = pl.ds(z, zn), pl.ds(y, yn)
    total = KEEP * w + R[zs, ys]
    for at, value in enumerate((x_prev(w), x_next(w), ym, yp, zm, zp)):
        total = total + A[at, zs, ys] * value
    put(total, z, y, zn, yn)


def put_padded(dst):
    def put(value, z, y, zn, yn):
        dst[pl.ds(z + 1, zn), pl.ds(y + 1, yn)] = value

    return put


def put_rows(dst, CY):
    def put(value, z, y, zn, yn):
        for i in range(zn):
            at = pl.multiple_of(((z + i) * CY + y) * 8, 8)
            dst[pl.ds(at, 8 * yn), :] = value[i].reshape(8 * yn, 128)

    return put


def by_row(ref):
    return ref.reshape(ref.shape[0], 1, 128)


def tangent_kernel(
    CZ, CY, cells_s, plane_s, cells_v, v_in, y_in, s_in, w_in, mu_out, v_out, reg_out, table,
    vin, yin, sin, weights, V, MU, DMU, REG, A, R, W1, W2, W3, T, rows0, rows1, held, parts,
    load, store, send, recv, sum_send, sum_recv,
):
    tiles = CY // 8
    loads = [
        pltpu.make_async_copy(src, dst, load.at[i])
        for i, (src, dst) in enumerate(
            ((v_in, vin), (y_in, yin), (s_in, sin), (w_in, weights))
        )
    ]
    for c in loads:
        c.start()
    faces = Faces(CZ, CY, send, recv)
    clear_faces((V, MU, DMU, W1, W2, W3), CZ, CY)
    greet(True)
    loads[0].wait()

    @pl.loop(0, CZ * tiles // 2)
    def _(j):
        for i in (2 * j, 2 * j + 1):
            z, y = i // tiles, (i % tiles) * 8
            for s in range(8):
                V[z + 1, y + 1 + s] = vin[i, pl.ds(s, 8, stride=8), :]

    faces.start(V, 0)
    loads[1].wait()
    loads[2].wait()

    def viscosity(z, t):
        i, y = z * tiles + t, t * 8
        here = pl.ds(y + 1, 8)
        c = V[z + 1, here]
        dz = V[z + 2, here] - c
        dy = V[z + 1, pl.ds(y + 2, 8)] - c
        dx = x_next(c, False) - c
        reg = lax.rsqrt((dz * dz + dy * dy + dx * dx) + 0.01)
        REG[z, pl.ds(y, 8)] = reg
        for s in range(8):
            MU[z + 1, y + 1 + s] = 1.0 + yin[i, pl.ds(s, 8, stride=8), :] * reg[s]
            DMU[z + 1, y + 1 + s] = sin[i, pl.ds(s, 8, stride=8), :] * reg[s]

    @pl.loop(0, CZ - 1)
    def _(z):
        for t in range(tiles - 1):
            viscosity(z, t)

    faces.arrive(V, 0)
    for t in range(tiles):
        viscosity(CZ - 1, t)

    pair = divisor(CZ - 1, 3)

    @pl.loop(0, (CZ - 1) // pair)
    def _(i):
        for j in range(pair):
            viscosity(i * pair + j, tiles - 1)

    faces.start(MU, 1)
    faces.start(DMU, 2)

    def source(z, y, zn, yn):
        zs, ys = pl.ds(z, zn), pl.ds(y, yn)
        face, dinv = coefficients(MU, z, y, zn, yn)
        for at in range(6):
            A[at, zs, ys] = face[at]
        d, *ds = around(DMU, z, y, zn, yn)
        v, *vs = around(V, z, y, zn, yn)
        ds += [x_prev(d, False), x_next(d, False)]
        vs += [x_prev(v, False), x_next(v, False)]
        total = (d + ds[0]) * (vs[0] - v)
        for dn, vn in zip(ds[1:], vs[1:]):
            total = total + (d + dn) * (vn - v)
        first = (0.5 * dinv) * total
        R[zs, ys] = first
        W1[pl.ds(z + 1, zn), pl.ds(y + 1, yn)] = first

    interior(CZ, CY, source, 1)
    faces.arrive(MU, 1)
    faces.arrive(DMU, 2)
    stores = [
        pltpu.make_async_copy(src, dst, store.at[i])
        for i, (src, dst) in enumerate(((MU, mu_out), (V, v_out), (REG, reg_out)))
    ]
    for c in stores:
        c.start()
    boundary_z(CZ, CY, source)
    faces.start(W1, 3, (0, 1))
    boundary_y(CZ, CY, source)
    faces.start(W1, 3, (2, 3))
    for step, (src, dst) in enumerate(((W1, W2), (W2, W3), (W3, None))):
        put = put_rows(T, CY) if dst is None else put_padded(dst)
        go = functools.partial(sweep, A, R, src, put)
        interior(CZ, CY, go, 2)
        faces.arrive(src, 3 + step)
        boundary_z(CZ, CY, go)
        if dst is not None:
            faces.start(dst, 4 + step, (0, 1))
        boundary_y(CZ, CY, go)
        if dst is not None:
            faces.start(dst, 4 + step, (2, 3))

    loads[3].wait()
    observe(cells_s, plane_s, cells_v, weights, T, parts, rows0, rows1)
    sum_all(parts, table, held, sum_send, sum_recv)
    for e, buf in enumerate((V, MU, DMU, W1, W2, W3)):
        faces.finish(buf, e)
    for c in stores:
        c.wait()


def adjoint_kernel(
    CZ, CY, q_in, mu_in, v_in, reg_in, out,
    Q, MU, V, REG, A, R, W1, W2, W3, W4, T, load, store, send, recv,
):
    loads = [
        pltpu.make_async_copy(src, dst, load.at[i])
        for i, (src, dst) in enumerate(((mu_in, MU), (q_in, Q), (v_in, V), (reg_in, REG)))
    ]
    for c in loads:
        c.start()
    faces = Faces(CZ, CY, send, recv)
    clear_faces((W1, W2, W3, W4), CZ, CY)
    greet(False)
    loads[0].wait()
    loads[1].wait()

    def begin(z, y, zn, yn):
        zs, ys = pl.ds(z, zn), pl.ds(y, yn)
        face, dinv = coefficients(MU, z, y, zn, yn)
        for at in range(6):
            A[at, zs, ys] = face[at]
        first = dinv * Q[zs, ys]
        R[zs, ys] = first
        W1[pl.ds(z + 1, zn), pl.ds(y + 1, yn)] = first

    def product(z, y, zn, yn):
        zs, ys = pl.ds(z, zn), pl.ds(y, yn)
        v, *vs = around(V, z, y, zn, yn)
        a, *many = around(W4, z, y, zn, yn)
        vs += [x_prev(v, False), x_next(v, False)]
        many += [x_prev(a, False), x_next(a, False)]
        total = (v - vs[0]) * (a - many[0])
        for vn, an in zip(vs[1:], many[1:]):
            total = total + (v - vn) * (a - an)
        total = (-0.5 * REG[zs, ys]) * total
        for i in range(zn):
            for j in range(yn):
                at = (z + i) * (CY // 8) + (y + j) // 8
                T[at, pl.ds((y + j) % 8, 8, stride=8), :] = total[i, j]

    boundary_z(CZ, CY, begin)
    faces.start(W1, 0, (0, 1))
    boundary_y(CZ, CY, begin)
    faces.start(W1, 0, (2, 3))
    interior(CZ, CY, begin, 1)
    for step, (src, dst) in enumerate(((W1, W2), (W2, W3), (W3, W4))):
        go = functools.partial(sweep, A, R, src, put_padded(dst))
        interior(CZ, CY, go, 2)
        faces.arrive(src, step)
        boundary_z(CZ, CY, go)
        faces.start(dst, step + 1, (0, 1))
        boundary_y(CZ, CY, go)
        faces.start(dst, step + 1, (2, 3))
    loads[2].wait()
    loads[3].wait()
    interior(CZ, CY, product, 1)
    faces.arrive(W4, 3)
    boundary_z(CZ, CY, product)
    boundary_y(CZ, CY, product)
    last = pltpu.make_async_copy(T, out, store)
    last.start()
    for e, buf in enumerate((W1, W2, W3, W4)):
        faces.finish(buf, e)
    last.wait()


def observe(cells_s, plane_s, cells_v, weights, field, parts, rows0, rows1):
    B, K = cells_s.shape
    step = cells_v.shape[1]
    sub, _ = ids((128, K))
    _, lane = ids((8, 128))

    def fetch(b, rows):
        for k in range(K):
            by_row(rows)[k] = by_row(field)[cells_s[b, k] >> 7]

    fetch(0, rows0)

    def group(g, acc):
        low, high = acc
        inner = cells_v[g] & 127
        for j in range(step):
            b = g * step + j
            rows, later = (rows0, rows1) if j % 2 == 0 else (rows1, rows0)
            fetch(jnp.minimum(b + 1, B - 1), later)
            hot = jnp.where(sub == inner[j : j + 1, :], 1.0, 0.0).T
            picked = rows[...] * hot
            main = picked.astype(BF16)
            rest = (picked - main.astype(F32)).astype(BF16)
            w = weights[b]
            both = jnp.dot(w, main, preferred_element_type=F32) + jnp.dot(
                w, rest, preferred_element_type=F32
            )
            total = jnp.sum(both, axis=1, keepdims=True)
            p = plane_s[b]
            p = jnp.where(p < PLANES, p, -1000)
            for n in range(3):
                low = low + jnp.where(lane == p + PLANES * n, total[8 * n : 8 * n + 8], 0.0)
            high = high + jnp.where(lane == p, total[24:32], 0.0)
        return low, high

    zero = jnp.zeros((8, 128), F32)
    low, high = lax.fori_loop(0, B // step, group, (zero, zero))
    parts[0, 0:8, :] = low
    parts[0, 8:16, :] = high


def sum_all(parts, out, held, send, recv):
    copies = []
    for at, (n, me, target) in enumerate(lines()):
        mine = []
        for d in range(1, n):
            c = pltpu.make_async_remote_copy(
                src_ref=parts.at[at],
                dst_ref=held.at[at, me],
                send_sem=send.at[at, d],
                recv_sem=recv.at[at, d],
                device_id=target(lax.rem(me + d, n)),
                device_id_type=MESH,
            )
            c.start()
            mine.append(c)
        held[at, me] = parts[at]
        for c in mine:
            c.wait_recv()
        total = held[at, 0]
        for i in range(1, n):
            total = total + held[at, i]
        if at < 3:
            parts[at + 1] = total
        else:
            out[...] = total
        copies += mine
    for c in copies:
        c.wait_send()


def scatter_kernel(B, K, copies, cells_s, plane_s, cells_v, weights, table, out, obs, values0, values1, *accs):
    size = out.shape[0]
    accs3 = [by_row(acc) for acc in accs]

    @pl.loop(0, size // 64)
    def _(i):
        for acc in accs:
            acc[pl.ds(pl.multiple_of(i * 64, 64), 64), :] = jnp.zeros((64, 128), F32)

    step = divisor(B, 8)
    sub, _ = ids((128, K))
    _, lane = ids((32, 128))
    packed = table[...]
    low = packed[0:8]
    po = jnp.concatenate(
        [low, pltpu.roll(low, 128 - PLANES, 1), pltpu.roll(low, 128 - 2 * PLANES, 1), packed[8:16]],
        axis=0,
    )
    po = jnp.where(lane < PLANES, po, 0.0)
    obs[...] = po[:, :PLANES]

    def spread(b, values):
        inner = cells_v[b // step] & 127
        row = jnp.zeros((1, K), jnp.int32)
        for j in range(step):
            row = jnp.where(b % step == j, inner[j : j + 1, :], row)
        mine = jnp.sum(jnp.where(lane == plane_s[b], po, 0.0), axis=1, keepdims=True)
        back = jnp.sum(weights[b].astype(F32) * mine, axis=0, keepdims=True)
        values[...] = jnp.where(sub == row, back, 0.0).T

    def add(b, values):
        for k in range(0, K, copies):
            at = [cells_s[b, k + j] >> 7 for j in range(copies)]
            new = [accs3[j][at[j]] + by_row(values)[k + j] for j in range(copies)]
            for j in range(copies):
                accs3[j][at[j]] = new[j]

    spread(0, values0)

    @pl.loop(0, B // 2)
    def _(i):
        spread(2 * i + 1, values1)
        add(2 * i, values0)
        spread(jnp.minimum(2 * i + 2, B - 1), values0)
        add(2 * i + 1, values1)

    @pl.loop(0, size // 64)
    def _(i):
        here = pl.ds(pl.multiple_of(i * 64, 64), 64)
        total = accs[0][here, :]
        for acc in accs[1:]:
            total = total + acc[here, :]
        out[here, :] = total


def shards(velocity, yield_stress, stress_step, block_weights, block_cells, block_plane):
    CZ, CY, NX = velocity.shape
    B, S, K = block_weights.shape
    core, padded = (CZ, CY, 8, 128), (CZ + 2, CY + 2, 8, 128)
    tiles = (CZ * CY // 8, 64, 128)

    def tiled(field):
        return field.reshape(CZ, CY // 8, 8, 8, 128).transpose(0, 1, 3, 2, 4).reshape(tiles)

    def sds(shape):
        return jax.ShapeDtypeStruct(shape, F32)

    def vm(shape):
        return pltpu.VMEM(shape, F32)

    def params(n=None):
        if n is None:
            return pltpu.CompilerParams(vmem_limit_bytes=LIMIT)
        return pltpu.CompilerParams(vmem_limit_bytes=LIMIT, collective_id=n, has_side_effects=True)

    DMA = pltpu.SemaphoreType.DMA
    groups = divisor(B, 8)
    cells_v = block_cells.reshape(B // groups, groups, K)
    mu, vel, reg, table = pl.pallas_call(
        functools.partial(tangent_kernel, CZ, CY),
        out_shape=(sds(padded), sds(padded), sds(core), sds((16, 128))),
        in_specs=[SMEM, SMEM, VMEM] + [ANY] * 4,
        out_specs=(ANY, ANY, ANY, VMEM),
        scratch_shapes=[vm(tiles)] * 3 + [pltpu.VMEM((B, S, K), BF16)]
        + [vm(padded)] * 3 + [vm(core), vm((6,) + core), vm(core)] + [vm(padded)] * 3
        + [vm((CZ * CY * 8, 128)), vm((K, 128)), vm((K, 128))]
        + [vm((4, 4, 16, 128)), vm((4, 16, 128))]
        + [DMA((4,)), DMA((3,)), DMA((6, 4)), DMA((6, 4)), DMA((4, 4)), DMA((4, 4))],
        compiler_params=params(0),
        name="tangent",
    )(
        block_cells, block_plane, cells_v,
        tiled(velocity), tiled(yield_stress), tiled(stress_step), block_weights,
    )

    copies = 8
    adj, obs = pl.pallas_call(
        functools.partial(scatter_kernel, B, K, copies),
        out_shape=(sds((CZ * CY * 8, 128)), sds((S, PLANES))),
        in_specs=[SMEM, SMEM, VMEM, VMEM, VMEM],
        out_specs=(VMEM, VMEM),
        scratch_shapes=[vm((K, 128))] * 2 + [vm((CZ * CY * 8, 128))] * copies,
        compiler_params=params(),
        name="scatter",
    )(block_cells, block_plane, cells_v, block_weights, table)

    product = pl.pallas_call(
        functools.partial(adjoint_kernel, CZ, CY),
        out_shape=sds(tiles),
        in_specs=[ANY] * 4,
        out_specs=ANY,
        scratch_shapes=[vm(core), vm(padded), vm(padded), vm(core), vm((6,) + core), vm(core)]
        + [vm(padded)] * 4 + [vm(tiles), DMA((4,)), DMA, DMA((4, 4)), DMA((4, 4))],
        compiler_params=params(1),
        name="adjoint",
    )(adj.reshape(core), mu, vel, reg)
    product = product.reshape(CZ, CY // 8, 8, 8, 128).transpose(0, 1, 3, 2, 4)
    return product.reshape(CZ, CY, NX), obs.T


def solution(mesh):
    placed = (
        P("gz", "xy", None),
        P("gz", "xy", None),
        P("gz", "xy", None),
        P(("gz", "xy"), None, None),
        P(("gz", "xy"), None),
        P(("gz", "xy")),
    )
    return jax.shard_map(
        shards, mesh=mesh, in_specs=placed, out_specs=(P("gz", "xy", None), P()), check_vma=False
    )
```

profile of v0, /device:TPU:32, one launch (start us, length us, event | category | flops | bytes accessed | tf_op | source)
XLA Modules:
  0.0 100.6 jit_solution(15051934697413936007)
XLA Ops:
  0.6 56.2 %tangent.1 = (f32[18,34,8,128]{3,2,1,0:T(8,128)}, f32[18,34,8,128]{3,2,1,0:T(8,128)}, f32[16,32,8,128]{3,2,1,0:T(8,128)}, f32[16,128]{1,0:T(8,128)}) custom-call(s32[64,128]{1,0:T(8,128)} %cells_s.3, s32[64]{0:T(128)} %plane_s.3, s32[8,8,128]{2,1,0:T(8,128)} %bitcast.28, f32[64,64,128]{2,1,0:T(8,128)} %bitcast.24, f32[64,64,128]{2,1,0:T(8,128)} %bitcast.25, ...), custom_call_target="tpu_custom_call" | custom-call | tf_op jit(solution)/shard_map/tangent/pallas_call | solution.py:564
  56.9 15.2 %scatter.1 = (f32[4096,128]{1,0:T(8,128)}, f32[32,40]{1,0:T(8,128)}) custom-call(s32[64,128]{1,0:T(8,128)} %cells_s.3, s32[64]{0:T(128)} %plane_s.3, s32[8,8,128]{2,1,0:T(8,128)} %bitcast.29, bf16[64,32,128]{2,1,0:T(8,128)(2,1)} %weights.1, f32[16,128]{1,0:T(8,128)} %get-tuple-element.8.table), custom_call_target="tpu_custom_call" | custom-call | tf_op jit(solution)/shard_map/scatter/pallas_call | solution.py:582
  72.1 25.3 %adjoint.1 = f32[64,64,128]{2,1,0:T(8,128)} custom-call(f32[16,32,8,128]{3,2,1,0:T(8,128)} %bitcast.27, f32[18,34,8,128]{3,2,1,0:T(8,128)} %get-tuple-element.10.mu_in, f32[18,34,8,128]{3,2,1,0:T(8,128)} %get-tuple-element.11.v_in, f32[16,32,8,128]{3,2,1,0:T(8,128)} %get-tuple-element.12.reg_in), custom_call_target="tpu_custom_call" | custom-call | tf_op jit(solution)/shard_map/adjoint/pallas_call | solution.py:592
  97.4 3.2 %copy.9 = f32[16,32,1024]{2,1,0:T(8,128)} copy(f32[16,32,1024]{2,1,0:T(8,128)} %bitcast.23) | data formatting | bytes 4194304
where the time goes:
time: 101 us
  Pallas kernels  96.8 us (96%)
  local copies, waits for them, and re-layouts  3.16 us (3%)
    pallas_call x1, Pallas kernels, shards(): pl.pallas_call(functools.partial(tangent_kernel, CZ, CY), out_shape=(sds(...  56.2 us
    pallas_call x1, Pallas kernels, shards(): pl.pallas_call(functools.partial(adjoint_kernel, CZ, CY), out_shape=sds(t...  25.3 us
    pallas_call x1, Pallas kernels, shards(): pl.pallas_call(functools.partial(scatter_kernel, B, K, copies), out_shape...  15.2 us
    unnamed x1, local copies, waits for them, and re-layouts  3.16 us

commit v1 on v0

--- a/solution.py
+++ b/solution.py
@@ -15,7 +15,9 @@
 VMEM = pl.BlockSpec(memory_space=pltpu.VMEM)
 SMEM = pl.BlockSpec(memory_space=pltpu.SMEM)
 ANY = pl.BlockSpec(memory_space=pl.ANY)
-LIMIT = 56 * 1024 * 1024
+HBM = pl.BlockSpec(memory_space=pltpu.HBM)
+MIB = 1024 * 1024
+BATCH = 16
 
 
 def ids(shape):
@@ -186,6 +188,10 @@
     )
 
 
+def regularized(dz, dy, dx):
+    return lax.rsqrt((dz * dz + dy * dy + dx * dx) + 0.01)
+
+
 def coefficients(MU, z, y, zn, yn):
     m, ym, yp, zm, zp = around(MU, z, y, zn, yn)
     xm, xp = x_prev(m, False), x_next(m, False)
@@ -235,15 +241,18 @@
 
 
 def tangent_kernel(
-    CZ, CY, cells_s, plane_s, cells_v, v_in, y_in, s_in, w_in, mu_out, v_out, reg_out, table,
-    vin, yin, sin, weights, V, MU, DMU, REG, A, R, W1, W2, W3, T, rows0, rows1, held, parts,
+    CZ, CY, c_in, p_in, q_in, v_in, y_in, s_in, w_in, mu_out, v_out, table,
+    cells_s, plane_s, cells_v, vin, yin, sin, weights, V, MU, DMU, A, R, W1, W2, W3, T, rows0, rows1, held, parts,
     load, store, send, recv, sum_send, sum_recv,
 ):
     tiles = CY // 8
     loads = [
         pltpu.make_async_copy(src, dst, load.at[i])
         for i, (src, dst) in enumerate(
-            ((v_in, vin), (y_in, yin), (s_in, sin), (w_in, weights))
+            (
+                (v_in, vin), (y_in, yin), (s_in, sin), (w_in, weights),
+                (c_in, cells_s), (p_in, plane_s), (q_in, cells_v),
+            )
         )
     ]
     for c in loads:
@@ -271,8 +280,7 @@
         dz = V[z + 2, here] - c
         dy = V[z + 1, pl.ds(y + 2, 8)] - c
         dx = x_next(c, False) - c
-        reg = lax.rsqrt((dz * dz + dy * dy + dx * dx) + 0.01)
-        REG[z, pl.ds(y, 8)] = reg
+        reg = regularized(dz, dy, dx)
         for s in range(8):
             MU[z + 1, y + 1 + s] = 1.0 + yin[i, pl.ds(s, 8, stride=8), :] * reg[s]
             DMU[z + 1, y + 1 + s] = sin[i, pl.ds(s, 8, stride=8), :] * reg[s]
@@ -317,7 +325,7 @@
     faces.arrive(DMU, 2)
     stores = [
         pltpu.make_async_copy(src, dst, store.at[i])
-        for i, (src, dst) in enumerate(((MU, mu_out), (V, v_out), (REG, reg_out)))
+        for i, (src, dst) in enumerate(((MU, mu_out), (V, v_out)))
     ]
     for c in stores:
         c.start()
@@ -337,8 +345,9 @@
         if dst is not None:
             faces.start(dst, 4 + step, (2, 3))
 
-    loads[3].wait()
-    observe(cells_s, plane_s, cells_v, weights, T, parts, rows0, rows1)
+    for c in loads[3:]:
+        c.wait()
+    observe(cells_s, plane_s, cells_v, weights, T, parts, (rows0, rows1))
     sum_all(parts, table, held, sum_send, sum_recv)
     for e, buf in enumerate((V, MU, DMU, W1, W2, W3)):
         faces.finish(buf, e)
@@ -347,12 +356,12 @@
 
 
 def adjoint_kernel(
-    CZ, CY, q_in, mu_in, v_in, reg_in, out,
-    Q, MU, V, REG, A, R, W1, W2, W3, W4, T, load, store, send, recv,
+    CZ, CY, q_in, mu_in, v_in, out,
+    Q, MU, V, A, R, W1, W2, W3, W4, T, load, store, send, recv,
 ):
     loads = [
         pltpu.make_async_copy(src, dst, load.at[i])
-        for i, (src, dst) in enumerate(((mu_in, MU), (q_in, Q), (v_in, V), (reg_in, REG)))
+        for i, (src, dst) in enumerate(((mu_in, MU), (q_in, Q), (v_in, V)))
     ]
     for c in loads:
         c.start()
@@ -380,11 +389,8 @@
         total = (v - vs[0]) * (a - many[0])
         for vn, an in zip(vs[1:], many[1:]):
             total = total + (v - vn) * (a - an)
-        total = (-0.5 * REG[zs, ys]) * total
-        for i in range(zn):
-            for j in range(yn):
-                at = (z + i) * (CY // 8) + (y + j) // 8
-                T[at, pl.ds((y + j) % 8, 8, stride=8), :] = total[i, j]
+        dy, dz, dx = vs[1] - v, vs[3] - v, vs[5] - v
+        T[zs, ys] = (-0.5 * regularized(dz, dy, dx)) * total
 
     boundary_z(CZ, CY, begin)
     faces.start(W1, 0, (0, 1))
@@ -400,7 +406,6 @@
         boundary_y(CZ, CY, go)
         faces.start(dst, step + 1, (2, 3))
     loads[2].wait()
-    loads[3].wait()
     interior(CZ, CY, product, 1)
     faces.arrive(W4, 3)
     boundary_z(CZ, CY, product)
@@ -412,34 +417,29 @@
     last.wait()
 
 
-def observe(cells_s, plane_s, cells_v, weights, field, parts, rows0, rows1):
+def observe(cells_s, plane_s, cells_v, weights, field, parts, rows):
     B, K = cells_s.shape
-    step = cells_v.shape[1]
+    group = rows[0].shape[0] // K
     sub, _ = ids((128, K))
     _, lane = ids((8, 128))
-
-    def fetch(b, rows):
-        for k in range(K):
-            by_row(rows)[k] = by_row(field)[cells_s[b, k] >> 7]
-
-    fetch(0, rows0)
-
-    def group(g, acc):
+    source = by_row(field)
+
+    def fetch(g, held):
+        target = by_row(held)
+        for j in range(group):
+            for k in range(0, K, BATCH):
+                got = [source[cells_s[g * group + j, k + i] >> 7] for i in range(BATCH)]
+                for i in range(BATCH):
+                    target[j * K + k + i] = got[i]
+
+    def share(g, held, acc):
         low, high = acc
         inner = cells_v[g] & 127
-        for j in range(step):
-            b = g * step + j
-            rows, later = (rows0, rows1) if j % 2 == 0 else (rows1, rows0)
-            fetch(jnp.minimum(b + 1, B - 1), later)
-            hot = jnp.where(sub == inner[j : j + 1, :], 1.0, 0.0).T
-            picked = rows[...] * hot
-            main = picked.astype(BF16)
-            rest = (picked - main.astype(F32)).astype(BF16)
-            w = weights[b]
-            both = jnp.dot(w, main, preferred_element_type=F32) + jnp.dot(
-                w, rest, preferred_element_type=F32
-            )
-            total = jnp.sum(both, axis=1, keepdims=True)
+        for j in range(group):
+            b = g * group + j
+            across = held[j * K : (j + 1) * K, :].T
+            cells = jnp.sum(jnp.where(sub == inner[j : j + 1, :], across, 0.0), axis=0, keepdims=True)
+            total = jnp.sum(weights[b].astype(F32) * cells, axis=1, keepdims=True)
             p = plane_s[b]
             p = jnp.where(p < PLANES, p, -1000)
             for n in range(3):
@@ -447,8 +447,16 @@
             high = high + jnp.where(lane == p, total[24:32], 0.0)
         return low, high
 
+    fetch(0, rows[0])
+
+    def body(i, acc):
+        fetch(2 * i + 1, rows[1])
+        acc = share(2 * i, rows[0], acc)
+        fetch(jnp.minimum(2 * i + 2, B // group - 1), rows[0])
+        return share(2 * i + 1, rows[1], acc)
+
     zero = jnp.zeros((8, 128), F32)
-    low, high = lax.fori_loop(0, B // step, group, (zero, zero))
+    low, high = lax.fori_loop(0, B // (2 * group), body, (zero, zero))
     parts[0, 0:8, :] = low
     parts[0, 8:16, :] = high
 
@@ -483,8 +491,21 @@
         c.wait_send()
 
 
-def scatter_kernel(B, K, copies, cells_s, plane_s, cells_v, weights, table, out, obs, values0, values1, *accs):
-    size = out.shape[0]
+def scatter_kernel(
+    copies, c_in, p_in, q_in, w_in, t_in, out, obs,
+    cells_s, plane_s, cells_v, weights, table, values0, values1, total, load, store, *accs,
+):
+    B, K = cells_s.shape
+    group = values0.shape[0] // K
+    size = total.shape[0]
+    loads = [
+        pltpu.make_async_copy(src, dst, load.at[i])
+        for i, (src, dst) in enumerate(
+            ((c_in, cells_s), (p_in, plane_s), (q_in, cells_v), (w_in, weights), (t_in, table))
+        )
+    ]
+    for c in loads:
+        c.start()
     accs3 = [by_row(acc) for acc in accs]
 
     @pl.loop(0, size // 64)
@@ -492,7 +513,8 @@
         for acc in accs:
             acc[pl.ds(pl.multiple_of(i * 64, 64), 64), :] = jnp.zeros((64, 128), F32)
 
-    step = divisor(B, 8)
+    for c in loads:
+        c.wait()
     sub, _ = ids((128, K))
     _, lane = ids((32, 128))
     packed = table[...]
@@ -504,38 +526,50 @@
     po = jnp.where(lane < PLANES, po, 0.0)
     obs[...] = po[:, :PLANES]
 
-    def spread(b, values):
-        inner = cells_v[b // step] & 127
-        row = jnp.zeros((1, K), jnp.int32)
-        for j in range(step):
-            row = jnp.where(b % step == j, inner[j : j + 1, :], row)
-        mine = jnp.sum(jnp.where(lane == plane_s[b], po, 0.0), axis=1, keepdims=True)
-        back = jnp.sum(weights[b].astype(F32) * mine, axis=0, keepdims=True)
-        values[...] = jnp.where(sub == row, back, 0.0).T
-
-    def add(b, values):
-        for k in range(0, K, copies):
-            at = [cells_s[b, k + j] >> 7 for j in range(copies)]
-            new = [accs3[j][at[j]] + by_row(values)[k + j] for j in range(copies)]
-            for j in range(copies):
-                accs3[j][at[j]] = new[j]
+    def spread(g, values):
+        inner = cells_v[g] & 127
+        for j in range(group):
+            b = g * group + j
+            mine = jnp.sum(jnp.where(lane == plane_s[b], po, 0.0), axis=1, keepdims=True)
+            back = jnp.sum(weights[b].astype(F32) * mine, axis=0, keepdims=True)
+            values[j * K : (j + 1) * K, :] = jnp.where(sub == inner[j : j + 1, :], back, 0.0).T
+
+    def add(g, values):
+        held = by_row(values)
+        for j in range(group):
+            for k in range(0, K, copies):
+                at = [cells_s[g * group + j, k + i] >> 7 for i in range(copies)]
+                new = [accs3[i][at[i]] + held[j * K + k + i] for i in range(copies)]
+                for i in range(copies):
+                    accs3[i][at[i]] = new[i]
 
     spread(0, values0)
 
-    @pl.loop(0, B // 2)
+    @pl.loop(0, B // (2 * group))
     def _(i):
         spread(2 * i + 1, values1)
         add(2 * i, values0)
-        spread(jnp.minimum(2 * i + 2, B - 1), values0)
+        spread(jnp.minimum(2 * i + 2, B // group - 1), values0)
         add(2 * i + 1, values1)
 
-    @pl.loop(0, size // 64)
-    def _(i):
-        here = pl.ds(pl.multiple_of(i * 64, 64), 64)
-        total = accs[0][here, :]
-        for acc in accs[1:]:
-            total = total + acc[here, :]
-        out[here, :] = total
+    parts = store.shape[0]
+    step = size // parts
+    stores = []
+    for n in range(parts):
+
+        @pl.loop(0, step // 64)
+        def _(i):
+            here = pl.ds(pl.multiple_of(n * step + i * 64, 64), 64)
+            value = accs[0][here, :]
+            for acc in accs[1:]:
+                value = value + acc[here, :]
+            total[here, :] = value
+
+        here = pl.ds(n * step, step)
+        stores.append(pltpu.make_async_copy(total.at[here], out.at[here], store.at[n]))
+        stores[-1].start()
+    for c in stores:
+        c.wait()
 
 
 def shards(velocity, yield_stress, stress_step, block_weights, block_cells, block_plane):
@@ -553,25 +587,30 @@
     def vm(shape):
         return pltpu.VMEM(shape, F32)
 
-    def params(n=None):
+    def params(limit, n=None):
         if n is None:
-            return pltpu.CompilerParams(vmem_limit_bytes=LIMIT)
-        return pltpu.CompilerParams(vmem_limit_bytes=LIMIT, collective_id=n, has_side_effects=True)
+            return pltpu.CompilerParams(vmem_limit_bytes=limit * MIB)
+        return pltpu.CompilerParams(
+            vmem_limit_bytes=limit * MIB, collective_id=n, has_side_effects=True
+        )
 
     DMA = pltpu.SemaphoreType.DMA
-    groups = divisor(B, 8)
-    cells_v = block_cells.reshape(B // groups, groups, K)
-    mu, vel, reg, table = pl.pallas_call(
+    group = divisor(B // 2, 4)
+    cells_v = block_cells.reshape(B // group, group, K)
+    small = [pltpu.SMEM((B, K), jnp.int32), pltpu.SMEM((B,), jnp.int32)]
+    small += [pltpu.VMEM(cells_v.shape, jnp.int32)]
+    held = [vm((group * K, 128))] * 2
+    mu, vel, table = pl.pallas_call(
         functools.partial(tangent_kernel, CZ, CY),
-        out_shape=(sds(padded), sds(padded), sds(core), sds((16, 128))),
-        in_specs=[SMEM, SMEM, VMEM] + [ANY] * 4,
-        out_specs=(ANY, ANY, ANY, VMEM),
-        scratch_shapes=[vm(tiles)] * 3 + [pltpu.VMEM((B, S, K), BF16)]
-        + [vm(padded)] * 3 + [vm(core), vm((6,) + core), vm(core)] + [vm(padded)] * 3
-        + [vm((CZ * CY * 8, 128)), vm((K, 128)), vm((K, 128))]
+        out_shape=(sds(padded), sds(padded), sds((16, 128))),
+        in_specs=[HBM] * 7,
+        out_specs=(ANY, ANY, VMEM),
+        scratch_shapes=small + [vm(tiles)] * 3 + [pltpu.VMEM((B, S, K), BF16)]
+        + [vm(padded)] * 3 + [vm((6,) + core), vm(core)] + [vm(padded)] * 3
+        + [vm((CZ * CY * 8, 128))] + held
         + [vm((4, 4, 16, 128)), vm((4, 16, 128))]
-        + [DMA((4,)), DMA((3,)), DMA((6, 4)), DMA((6, 4)), DMA((4, 4)), DMA((4, 4))],
-        compiler_params=params(0),
+        + [DMA((7,)), DMA((2,)), DMA((6, 4)), DMA((6, 4)), DMA((4, 4)), DMA((4, 4))],
+        compiler_params=params(56, 0),
         name="tangent",
     )(
         block_cells, block_plane, cells_v,
@@ -580,26 +619,27 @@
 
     copies = 8
     adj, obs = pl.pallas_call(
-        functools.partial(scatter_kernel, B, K, copies),
+        functools.partial(scatter_kernel, copies),
         out_shape=(sds((CZ * CY * 8, 128)), sds((S, PLANES))),
-        in_specs=[SMEM, SMEM, VMEM, VMEM, VMEM],
-        out_specs=(VMEM, VMEM),
-        scratch_shapes=[vm((K, 128))] * 2 + [vm((CZ * CY * 8, 128))] * copies,
-        compiler_params=params(),
+        in_specs=[HBM] * 4 + [ANY],
+        out_specs=(ANY, VMEM),
+        scratch_shapes=small + [pltpu.VMEM((B, S, K), BF16), vm((16, 128))] + held
+        + [vm((CZ * CY * 8, 128)), DMA((5,)), DMA((4,))]
+        + [vm((CZ * CY * 8, 128))] * copies,
+        compiler_params=params(24),
         name="scatter",
     )(block_cells, block_plane, cells_v, block_weights, table)
 
     product = pl.pallas_call(
         functools.partial(adjoint_kernel, CZ, CY),
-        out_shape=sds(tiles),
-        in_specs=[ANY] * 4,
+        out_shape=sds(core),
+        in_specs=[ANY] * 3,
         out_specs=ANY,
-        scratch_shapes=[vm(core), vm(padded), vm(padded), vm(core), vm((6,) + core), vm(core)]
-        + [vm(padded)] * 4 + [vm(tiles), DMA((4,)), DMA, DMA((4, 4)), DMA((4, 4))],
-        compiler_params=params(1),
+        scratch_shapes=[vm(core), vm(padded), vm(padded), vm((6,) + core), vm(core)]
+        + [vm(padded)] * 4 + [vm(core), DMA((3,)), DMA, DMA((4, 4)), DMA((4, 4))],
+        compiler_params=params(48, 1),
         name="adjoint",
-    )(adj.reshape(core), mu, vel, reg)
-    product = product.reshape(CZ, CY // 8, 8, 8, 128).transpose(0, 1, 3, 2, 4)
+    )(adj.reshape(core), mu, vel)
     return product.reshape(CZ, CY, NX), obs.T
 
 

time: 101 us -> 98.7 us (0.977)
  Pallas kernels: 96.8 us -> 95.7 us
    unnamed x1 -> x8, local copies, waits for them, and re-layouts: 3.16 us -> 0.7 us
    pallas_call x1, Pallas kernels: 56.2 us -> 54.5 us  [shards(): pl.pallas_call(functools.partial(tangent_kernel, CZ, CY), out_shape=(sds(...]
    reshape x0 -> x1, local copies, waits for them, and re-layouts: none -> 1.49 us  [shards(): return (product.reshape(CZ, CY, NX), obs.T)]
where the time goes in v1:
time: 98.7 us; the launch traced here: 98.6 us
  Pallas kernels  95.7 us (97%)
  local copies, waits for them, and re-layouts  2.19 us (2%)
    pallas_call x1, Pallas kernels, shards(): pl.pallas_call(functools.partial(tangent_kernel, CZ, CY), out_shape=(sds(...  54.5 us
    pallas_call x1, Pallas kernels, shards(): pl.pallas_call(functools.partial(adjoint_kernel, CZ, CY), out_shape=sds(c...  24 us
    pallas_call x1, Pallas kernels, shards(): pl.pallas_call(functools.partial(scatter_kernel, copies), out_shape=(sds(...  17.2 us

profile of v1, /device:TPU:32, one launch (start us, length us, event | category | flops | bytes accessed | tf_op | source)
XLA Modules:
  0.0 98.6 jit_solution(8534044249167230608)
XLA Ops:
  0.6 0.0 copy-start
  0.6 0.0 copy-start.1
  0.7 0.0 copy-start.3
  0.7 54.5 %tangent.1 = (f32[18,34,8,128]{3,2,1,0:T(8,128)}, f32[18,34,8,128]{3,2,1,0:T(8,128)}, f32[16,128]{1,0:T(8,128)}) custom-call(s32[64,128]{1,0:T(8,128)} %c_in.3, s32[64]{0:T(128)} %p_in.3, s32[16,4,128]{2,1,0:T(4,128)} %bitcast.21, f32[64,64,128]{2,1,0:T(8,128)} %bitcast.23, f32[64,64,128]{2,1,0:T(8,128)} %bitcast.24, f32[64,64,128]{2,1,0:T(8,128)} %bitcast.25, ...), custom_call_target="tpu_custom_call" | custom-call | tf_op jit(solution)/shard_map/tangent/pallas_call | solution.py:603
  55.2 0.0 copy-done
  55.2 0.0 copy-done.1
  55.2 0.0 copy-done.3
  55.2 0.0 copy-start.2
  55.2 0.7 copy-done.2
  55.9 17.2 %scatter.1 = (f32[4096,128]{1,0:T(8,128)S(1)}, f32[32,40]{1,0:T(8,128)}) custom-call(s32[64,128]{1,0:T(8,128)S(1)} %copy-done.1, s32[64]{0:T(128)S(1)} %copy-done.3, s32[16,4,128]{2,1,0:T(4,128)S(1)} %bitcast.22, bf16[64,32,128]{2,1,0:T(8,128)(2,1)S(1)} %copy-done, f32[16,128]{1,0:T(8,128)S(1)} %copy-done.2), custom_call_target="tpu_custom_call" | custom-call | tf_op jit(solution)/shard_map/scatter/pallas_call | solution.py:621
  73.1 24.0 %adjoint.1 = f32[16,32,8,128]{3,2,1,0:T(8,128)S(1)} custom-call(f32[16,32,8,128]{3,2,1,0:T(8,128)S(1)} %bitcast.20, f32[18,34,8,128]{3,2,1,0:T(8,128)} %get-tuple-element.9.mu_in, f32[18,34,8,128]{3,2,1,0:T(8,128)} %get-tuple-element.10.v_in), custom_call_target="tpu_custom_call" | custom-call | tf_op jit(solution)/shard_map/adjoint/pallas_call | solution.py:633
  97.1 1.5 %reshape.39 = f32[16,32,1024]{2,1,0:T(8,128)} reshape(f32[16,32,8,128]{3,2,1,0:T(8,128)S(1)} %adjoint.1) | data formatting | bytes 4194304 | tf_op jit(solution)/shard_map/reshape | solution.py:643
Async XLA Ops:
  0.6 54.6 %copy-start = (bf16[64,32,128]{2,1,0:T(8,128)(2,1)S(1)}, bf16[64,32,128]{2,1,0:T(8,128)(2,1)}, u32[]{:S(2)}) copy-start(bf16[64,32,128]{2,1,0:T(8,128)(2,1)} %w_in.3) | copy-start | bytes 1572868
  0.6 54.6 %copy-start.1 = (s32[64,128]{1,0:T(8,128)S(1)}, s32[64,128]{1,0:T(8,128)}, u32[]{:S(2)}) copy-start(s32[64,128]{1,0:T(8,128)} %c_in.3) | copy-start | bytes 98308
  0.7 54.6 %copy-start.3 = (s32[64]{0:T(128)S(1)}, s32[64]{0:T(128)}, u32[]{:S(2)}) copy-start(s32[64]{0:T(128)} %p_in.3) | copy-start | bytes 772
  55.2 0.7 copy-start.2

commit v2 on v1

--- a/solution.py
+++ b/solution.py
@@ -97,8 +97,7 @@
     g, x = lax.axis_index("gz"), lax.axis_index("xy")
     across = min(X, 4)
     return (
-        (2, g % 2, lambda t: ((g // 2) * 2 + t, x)),
-        (G // 2, g // 2, lambda t: (t * 2 + g % 2, x)),
+        (G, g, lambda t: (t, x)),
         (across, x % across, lambda t: (g, (x // across) * across + t)),
         (X // across, x // across, lambda t: (g, t * across + x % across)),
     )
@@ -241,8 +240,8 @@
 
 
 def tangent_kernel(
-    CZ, CY, c_in, p_in, q_in, v_in, y_in, s_in, w_in, mu_out, v_out, table,
-    cells_s, plane_s, cells_v, vin, yin, sin, weights, V, MU, DMU, A, R, W1, W2, W3, T, rows0, rows1, held, parts,
+    CZ, CY, c_in, p_in, v_in, y_in, s_in, w_in, mu_out, v_out, rows_out, table,
+    rows_s, plane_s, cells_v, rows_v, vin, yin, sin, weights, V, MU, DMU, A, R, W1, W2, W3, T, rows0, rows1, held, parts,
     load, store, send, recv, sum_send, sum_recv,
 ):
     tiles = CY // 8
@@ -251,7 +250,7 @@
         for i, (src, dst) in enumerate(
             (
                 (v_in, vin), (y_in, yin), (s_in, sin), (w_in, weights),
-                (c_in, cells_s), (p_in, plane_s), (q_in, cells_v),
+                (c_in, cells_v), (p_in, plane_s),
             )
         )
     ]
@@ -303,6 +302,14 @@
 
     faces.start(MU, 1)
     faces.start(DMU, 2)
+    loads[4].wait()
+    rows_v[...] = cells_v[...] >> 7
+    numbers = [
+        pltpu.make_async_copy(rows_v, dst, store.at[2 + i])
+        for i, dst in enumerate((rows_s, rows_out))
+    ]
+    for c in numbers:
+        c.start()
 
     def source(z, y, zn, yn):
         zs, ys = pl.ds(z, zn), pl.ds(y, yn)
@@ -345,13 +352,14 @@
         if dst is not None:
             faces.start(dst, 4 + step, (2, 3))
 
-    for c in loads[3:]:
-        c.wait()
-    observe(cells_s, plane_s, cells_v, weights, T, parts, (rows0, rows1))
+    loads[3].wait()
+    loads[5].wait()
+    numbers[0].wait()
+    observe(rows_s, plane_s, cells_v, weights, T, parts, (rows0, rows1))
     sum_all(parts, table, held, sum_send, sum_recv)
     for e, buf in enumerate((V, MU, DMU, W1, W2, W3)):
         faces.finish(buf, e)
-    for c in stores:
+    for c in stores + numbers[1:]:
         c.wait()
 
 
@@ -417,8 +425,8 @@
     last.wait()
 
 
-def observe(cells_s, plane_s, cells_v, weights, field, parts, rows):
-    B, K = cells_s.shape
+def observe(rows_s, plane_s, cells_v, weights, field, parts, rows):
+    B, K = rows_s.shape
     group = rows[0].shape[0] // K
     sub, _ = ids((128, K))
     _, lane = ids((8, 128))
@@ -428,17 +436,17 @@
         target = by_row(held)
         for j in range(group):
             for k in range(0, K, BATCH):
-                got = [source[cells_s[g * group + j, k + i] >> 7] for i in range(BATCH)]
+                got = [source[rows_s[g * group + j, k + i]] for i in range(BATCH)]
                 for i in range(BATCH):
                     target[j * K + k + i] = got[i]
 
     def share(g, held, acc):
         low, high = acc
-        inner = cells_v[g] & 127
         for j in range(group):
             b = g * group + j
+            inner = by_row(cells_v)[b] & 127
             across = held[j * K : (j + 1) * K, :].T
-            cells = jnp.sum(jnp.where(sub == inner[j : j + 1, :], across, 0.0), axis=0, keepdims=True)
+            cells = jnp.sum(jnp.where(sub == inner, across, 0.0), axis=0, keepdims=True)
             total = jnp.sum(weights[b].astype(F32) * cells, axis=1, keepdims=True)
             p = plane_s[b]
             p = jnp.where(p < PLANES, p, -1000)
@@ -482,7 +490,7 @@
         total = held[at, 0]
         for i in range(1, n):
             total = total + held[at, i]
-        if at < 3:
+        if at < 2:
             parts[at + 1] = total
         else:
             out[...] = total
@@ -491,21 +499,10 @@
         c.wait_send()
 
 
-def scatter_kernel(
-    copies, c_in, p_in, q_in, w_in, t_in, out, obs,
-    cells_s, plane_s, cells_v, weights, table, values0, values1, total, load, store, *accs,
-):
-    B, K = cells_s.shape
+def scatter_kernel(copies, rows_s, plane_s, cells_v, weights, table, out, obs, values0, values1, *accs):
+    B, K = rows_s.shape
     group = values0.shape[0] // K
-    size = total.shape[0]
-    loads = [
-        pltpu.make_async_copy(src, dst, load.at[i])
-        for i, (src, dst) in enumerate(
-            ((c_in, cells_s), (p_in, plane_s), (q_in, cells_v), (w_in, weights), (t_in, table))
-        )
-    ]
-    for c in loads:
-        c.start()
+    size = out.shape[0]
     accs3 = [by_row(acc) for acc in accs]
 
     @pl.loop(0, size // 64)
@@ -513,8 +510,6 @@
         for acc in accs:
             acc[pl.ds(pl.multiple_of(i * 64, 64), 64), :] = jnp.zeros((64, 128), F32)
 
-    for c in loads:
-        c.wait()
     sub, _ = ids((128, K))
     _, lane = ids((32, 128))
     packed = table[...]
@@ -527,18 +522,18 @@
     obs[...] = po[:, :PLANES]
 
     def spread(g, values):
-        inner = cells_v[g] & 127
         for j in range(group):
             b = g * group + j
+            inner = by_row(cells_v)[b] & 127
             mine = jnp.sum(jnp.where(lane == plane_s[b], po, 0.0), axis=1, keepdims=True)
             back = jnp.sum(weights[b].astype(F32) * mine, axis=0, keepdims=True)
-            values[j * K : (j + 1) * K, :] = jnp.where(sub == inner[j : j + 1, :], back, 0.0).T
+            values[j * K : (j + 1) * K, :] = jnp.where(sub == inner, back, 0.0).T
 
     def add(g, values):
         held = by_row(values)
         for j in range(group):
             for k in range(0, K, copies):
-                at = [cells_s[g * group + j, k + i] >> 7 for i in range(copies)]
+                at = [rows_s[g * group + j, k + i] for i in range(copies)]
                 new = [accs3[i][at[i]] + held[j * K + k + i] for i in range(copies)]
                 for i in range(copies):
                     accs3[i][at[i]] = new[i]
@@ -552,24 +547,13 @@
         spread(jnp.minimum(2 * i + 2, B // group - 1), values0)
         add(2 * i + 1, values1)
 
-    parts = store.shape[0]
-    step = size // parts
-    stores = []
-    for n in range(parts):
-
-        @pl.loop(0, step // 64)
-        def _(i):
-            here = pl.ds(pl.multiple_of(n * step + i * 64, 64), 64)
-            value = accs[0][here, :]
-            for acc in accs[1:]:
-                value = value + acc[here, :]
-            total[here, :] = value
-
-        here = pl.ds(n * step, step)
-        stores.append(pltpu.make_async_copy(total.at[here], out.at[here], store.at[n]))
-        stores[-1].start()
-    for c in stores:
-        c.wait()
+    @pl.loop(0, size // 64)
+    def _(i):
+        here = pl.ds(pl.multiple_of(i * 64, 64), 64)
+        value = accs[0][here, :]
+        for acc in accs[1:]:
+            value = value + acc[here, :]
+        out[here, :] = value
 
 
 def shards(velocity, yield_stress, stress_step, block_weights, block_cells, block_plane):
@@ -595,25 +579,23 @@
         )
 
     DMA = pltpu.SemaphoreType.DMA
-    group = divisor(B // 2, 4)
-    cells_v = block_cells.reshape(B // group, group, K)
-    small = [pltpu.SMEM((B, K), jnp.int32), pltpu.SMEM((B,), jnp.int32)]
-    small += [pltpu.VMEM(cells_v.shape, jnp.int32)]
-    held = [vm((group * K, 128))] * 2
-    mu, vel, table = pl.pallas_call(
+    numbers = jax.ShapeDtypeStruct((B, K), jnp.int32)
+    held = [vm((K, 128))] * 2
+    mu, vel, rows, table = pl.pallas_call(
         functools.partial(tangent_kernel, CZ, CY),
-        out_shape=(sds(padded), sds(padded), sds((16, 128))),
-        in_specs=[HBM] * 7,
-        out_specs=(ANY, ANY, VMEM),
-        scratch_shapes=small + [vm(tiles)] * 3 + [pltpu.VMEM((B, S, K), BF16)]
+        out_shape=(sds(padded), sds(padded), numbers, sds((16, 128))),
+        in_specs=[HBM] * 6,
+        out_specs=(ANY, ANY, ANY, VMEM),
+        scratch_shapes=[pltpu.SMEM((B, K), jnp.int32), pltpu.SMEM((B,), jnp.int32)]
+        + [pltpu.VMEM((B, K), jnp.int32)] * 2 + [vm(tiles)] * 3 + [pltpu.VMEM((B, S, K), BF16)]
         + [vm(padded)] * 3 + [vm((6,) + core), vm(core)] + [vm(padded)] * 3
         + [vm((CZ * CY * 8, 128))] + held
-        + [vm((4, 4, 16, 128)), vm((4, 16, 128))]
-        + [DMA((7,)), DMA((2,)), DMA((6, 4)), DMA((6, 4)), DMA((4, 4)), DMA((4, 4))],
+        + [vm((3, 8, 16, 128)), vm((3, 16, 128))]
+        + [DMA((6,)), DMA((4,)), DMA((6, 4)), DMA((6, 4)), DMA((3, 8)), DMA((3, 8))],
         compiler_params=params(56, 0),
         name="tangent",
     )(
-        block_cells, block_plane, cells_v,
+        block_cells, block_plane,
         tiled(velocity), tiled(yield_stress), tiled(stress_step), block_weights,
     )
 
@@ -621,14 +603,12 @@
     adj, obs = pl.pallas_call(
         functools.partial(scatter_kernel, copies),
         out_shape=(sds((CZ * CY * 8, 128)), sds((S, PLANES))),
-        in_specs=[HBM] * 4 + [ANY],
-        out_specs=(ANY, VMEM),
-        scratch_shapes=small + [pltpu.VMEM((B, S, K), BF16), vm((16, 128))] + held
-        + [vm((CZ * CY * 8, 128)), DMA((5,)), DMA((4,))]
-        + [vm((CZ * CY * 8, 128))] * copies,
+        in_specs=[SMEM, SMEM, VMEM, VMEM, VMEM],
+        out_specs=(VMEM, VMEM),
+        scratch_shapes=held + [vm((CZ * CY * 8, 128))] * copies,
         compiler_params=params(24),
         name="scatter",
-    )(block_cells, block_plane, cells_v, block_weights, table)
+    )(rows, block_plane, block_cells, block_weights, table)
 
     product = pl.pallas_call(
         functools.partial(adjoint_kernel, CZ, CY),

time: 98.7 us -> 97.3 us (0.986)
  Pallas kernels: 95.7 us -> 93.4 us
    pallas_call x1, Pallas kernels: 17.2 us -> 12.8 us  [shards(): pl.pallas_call(functools.partial(scatter_kernel, copies), out_shape=(sds(...]
    pallas_call x1, Pallas kernels: 54.5 us -> 56.5 us  [shards(): pl.pallas_call(functools.partial(tangent_kernel, CZ, CY), out_shape=(sds(...]
where the time goes in v2:
time: 97.3 us; the launch traced here: 97 us
  Pallas kernels  93.4 us (96%)
  local copies, waits for them, and re-layouts  2.95 us (3%)
    pallas_call x1, Pallas kernels, shards(): pl.pallas_call(functools.partial(tangent_kernel, CZ, CY), out_shape=(sds(...  56.5 us
    pallas_call x1, Pallas kernels, shards(): pl.pallas_call(functools.partial(adjoint_kernel, CZ, CY), out_shape=sds(c...  24 us
    pallas_call x1, Pallas kernels, shards(): pl.pallas_call(functools.partial(scatter_kernel, copies), out_shape=(sds(...  12.8 us

profile of v2, /device:TPU:32, one launch (start us, length us, event | category | flops | bytes accessed | tf_op | source)
XLA Modules:
  0.0 97.0 jit_solution(10595625915759309347)
XLA Ops:
  0.6 0.0 copy-start
  0.6 0.0 copy-start.1
  0.7 0.0 copy-start.4
  0.7 56.5 %tangent.1 = (f32[18,34,8,128]{3,2,1,0:T(8,128)}, f32[18,34,8,128]{3,2,1,0:T(8,128)}, s32[64,128]{1,0:T(8,128)}, f32[16,128]{1,0:T(8,128)}) custom-call(s32[64,128]{1,0:T(8,128)} %cells_v.1, s32[64]{0:T(128)} %plane_s.1, f32[64,64,128]{2,1,0:T(8,128)} %bitcast.20, f32[64,64,128]{2,1,0:T(8,128)} %bitcast.21, f32[64,64,128]{2,1,0:T(8,128)} %bitcast.22, ...), custom_call_target="tpu_custom_call" | custom-call | tf_op jit(solution)/shard_map/tangent/pallas_call | solution.py:584
  57.2 0.0 copy-done
  57.2 0.0 copy-done.1
  57.2 0.0 copy-done.4
  57.2 0.0 copy-start.2
  57.2 0.7 copy-done.2
  58.0 0.0 copy-start.3
  58.0 0.7 copy-done.3
  58.7 12.8 %scatter.1 = (f32[4096,128]{1,0:T(8,128)S(1)}, f32[32,40]{1,0:T(8,128)}) custom-call(s32[64,128]{1,0:T(8,128)S(1)} %copy-done.2, s32[64]{0:T(128)S(1)} %copy-done.4, s32[64,128]{1,0:T(8,128)S(1)} %copy-done.1, bf16[64,32,128]{2,1,0:T(8,128)(2,1)S(1)} %copy-done, f32[16,128]{1,0:T(8,128)S(1)} %copy-done.3), custom_call_target="tpu_custom_call" | custom-call | tf_op jit(solution)/shard_map/scatter/pallas_call | solution.py:603
  71.5 24.0 %adjoint.1 = f32[16,32,8,128]{3,2,1,0:T(8,128)S(1)} custom-call(f32[16,32,8,128]{3,2,1,0:T(8,128)S(1)} %bitcast.19, f32[18,34,8,128]{3,2,1,0:T(8,128)} %get-tuple-element.11.mu_in, f32[18,34,8,128]{3,2,1,0:T(8,128)} %get-tuple-element.12.v_in), custom_call_target="tpu_custom_call" | custom-call | tf_op jit(solution)/shard_map/adjoint/pallas_call | solution.py:613
  95.6 1.5 %reshape.35 = f32[16,32,1024]{2,1,0:T(8,128)} reshape(f32[16,32,8,128]{3,2,1,0:T(8,128)S(1)} %adjoint.1) | data formatting | bytes 4194304 | tf_op jit(solution)/shard_map/reshape | solution.py:623
Async XLA Ops:
  0.6 56.6 %copy-start = (bf16[64,32,128]{2,1,0:T(8,128)(2,1)S(1)}, bf16[64,32,128]{2,1,0:T(8,128)(2,1)}, u32[]{:S(2)}) copy-start(bf16[64,32,128]{2,1,0:T(8,128)(2,1)} %weights.1) | copy-start | bytes 1572868
  0.6 56.6 %copy-start.1 = (s32[64,128]{1,0:T(8,128)S(1)}, s32[64,128]{1,0:T(8,128)}, u32[]{:S(2)}) copy-start(s32[64,128]{1,0:T(8,128)} %cells_v.1) | copy-start | bytes 98308
  0.7 56.6 %copy-start.4 = (s32[64]{0:T(128)S(1)}, s32[64]{0:T(128)}, u32[]{:S(2)}) copy-start(s32[64]{0:T(128)} %plane_s.1) | copy-start | bytes 772
  57.2 0.8 copy-start.2
  58.0 0.7 copy-start.3

commit v3 on v2

--- a/solution.py
+++ b/solution.py
@@ -70,12 +70,14 @@
             device_id_type=MESH,
         )
 
-    def start(self, buf, e, which=(0, 1, 2, 3)):
-        for d in which:
-
-            @pl.when(self.has[d])
-            def _():
-                self.copy(buf, e, d).start()
+    def leave(self, buf, e, d):
+        @pl.when(self.has[d])
+        def _():
+            self.copy(buf, e, d).start()
+
+    def start(self, buf, e):
+        for d in range(4):
+            self.leave(buf, e, d)
 
     def arrive(self, buf, e):
         for d in range(4):
@@ -150,20 +152,18 @@
                 f(1 + i * planes + p, y, 1, yn)
 
 
-def boundary_z(CZ, CY, f):
-    yn = divisor(CY, 8)
-
-    @pl.loop(0, 2)
-    def _(i):
+def boundary(CZ, CY, f, leave=None):
+    yn, zn = divisor(CY, 8), divisor(CZ - 2, 8)
+    for d, z in enumerate((0, CZ - 1)):
         for y in range(0, CY, yn):
-            f(i * (CZ - 1), y, 1, yn)
-
-
-def boundary_y(CZ, CY, f):
-    zn = divisor(CZ - 2, 8)
-    for y in (0, CY - 1):
+            f(z, y, 1, yn)
+        if leave:
+            leave(d)
+    for d, y in enumerate((0, CY - 1)):
         for z in range(1, CZ - 1, zn):
             f(z, y, zn, 1)
+        if leave:
+            leave(2 + d)
 
 
 def around(ref, z, y, zn, yn):
@@ -336,21 +336,13 @@
     ]
     for c in stores:
         c.start()
-    boundary_z(CZ, CY, source)
-    faces.start(W1, 3, (0, 1))
-    boundary_y(CZ, CY, source)
-    faces.start(W1, 3, (2, 3))
+    boundary(CZ, CY, source, functools.partial(faces.leave, W1, 3))
     for step, (src, dst) in enumerate(((W1, W2), (W2, W3), (W3, None))):
         put = put_rows(T, CY) if dst is None else put_padded(dst)
         go = functools.partial(sweep, A, R, src, put)
         interior(CZ, CY, go, 2)
         faces.arrive(src, 3 + step)
-        boundary_z(CZ, CY, go)
-        if dst is not None:
-            faces.start(dst, 4 + step, (0, 1))
-        boundary_y(CZ, CY, go)
-        if dst is not None:
-            faces.start(dst, 4 + step, (2, 3))
+        boundary(CZ, CY, go, dst is not None and functools.partial(faces.leave, dst, 4 + step))
 
     loads[3].wait()
     loads[5].wait()
@@ -400,24 +392,17 @@
         dy, dz, dx = vs[1] - v, vs[3] - v, vs[5] - v
         T[zs, ys] = (-0.5 * regularized(dz, dy, dx)) * total
 
-    boundary_z(CZ, CY, begin)
-    faces.start(W1, 0, (0, 1))
-    boundary_y(CZ, CY, begin)
-    faces.start(W1, 0, (2, 3))
+    boundary(CZ, CY, begin, functools.partial(faces.leave, W1, 0))
     interior(CZ, CY, begin, 1)
     for step, (src, dst) in enumerate(((W1, W2), (W2, W3), (W3, W4))):
         go = functools.partial(sweep, A, R, src, put_padded(dst))
         interior(CZ, CY, go, 2)
         faces.arrive(src, step)
-        boundary_z(CZ, CY, go)
-        faces.start(dst, step + 1, (0, 1))
-        boundary_y(CZ, CY, go)
-        faces.start(dst, step + 1, (2, 3))
+        boundary(CZ, CY, go, functools.partial(faces.leave, dst, step + 1))
     loads[2].wait()
     interior(CZ, CY, product, 1)
     faces.arrive(W4, 3)
-    boundary_z(CZ, CY, product)
-    boundary_y(CZ, CY, product)
+    boundary(CZ, CY, product)
     last = pltpu.make_async_copy(T, out, store)
     last.start()
     for e, buf in enumerate((W1, W2, W3, W4)):
@@ -458,10 +443,11 @@
     fetch(0, rows[0])
 
     def body(i, acc):
+        acc = share(2 * i, rows[0], acc)
         fetch(2 * i + 1, rows[1])
-        acc = share(2 * i, rows[0], acc)
+        acc = share(2 * i + 1, rows[1], acc)
         fetch(jnp.minimum(2 * i + 2, B // group - 1), rows[0])
-        return share(2 * i + 1, rows[1], acc)
+        return acc
 
     zero = jnp.zeros((8, 128), F32)
     low, high = lax.fori_loop(0, B // (2 * group), body, (zero, zero))
@@ -580,7 +566,7 @@
 
     DMA = pltpu.SemaphoreType.DMA
     numbers = jax.ShapeDtypeStruct((B, K), jnp.int32)
-    held = [vm((K, 128))] * 2
+    held, spare = [vm((divisor(B // 2, 4) * K, 128))] * 2, [vm((divisor(B // 2, 2) * K, 128))] * 2
     mu, vel, rows, table = pl.pallas_call(
         functools.partial(tangent_kernel, CZ, CY),
         out_shape=(sds(padded), sds(padded), numbers, sds((16, 128))),
@@ -605,7 +591,7 @@
         out_shape=(sds((CZ * CY * 8, 128)), sds((S, PLANES))),
         in_specs=[SMEM, SMEM, VMEM, VMEM, VMEM],
         out_specs=(VMEM, VMEM),
-        scratch_shapes=held + [vm((CZ * CY * 8, 128))] * copies,
+        scratch_shapes=spare + [vm((CZ * CY * 8, 128))] * copies,
         compiler_params=params(24),
         name="scatter",
     )(rows, block_plane, block_cells, block_weights, table)

time: 97.3 us -> 94.5 us (0.971)
  Pallas kernels: 93.4 us -> 90.6 us
    pallas_call x1, Pallas kernels: 56.5 us -> 52.5 us  [shards(): pl.pallas_call(functools.partial(tangent_kernel, CZ, CY), out_shape=(sds(...]
    pallas_call x1, Pallas kernels: 12.8 us -> 14 us  [shards(): pl.pallas_call(functools.partial(scatter_kernel, copies), out_shape=(sds(...]
where the time goes in v3:
time: 94.5 us; the launch traced here: 94.3 us
  Pallas kernels  90.6 us (96%)
  local copies, waits for them, and re-layouts  2.95 us (3%)
    pallas_call x1, Pallas kernels, shards(): pl.pallas_call(functools.partial(tangent_kernel, CZ, CY), out_shape=(sds(...  52.5 us
    pallas_call x1, Pallas kernels, shards(): pl.pallas_call(functools.partial(adjoint_kernel, CZ, CY), out_shape=sds(c...  24.1 us
    pallas_call x1, Pallas kernels, shards(): pl.pallas_call(functools.partial(scatter_kernel, copies), out_shape=(sds(...  14 us

profile of v3, /device:TPU:32, one launch (start us, length us, event | category | flops | bytes accessed | tf_op | source)
XLA Modules:
  0.0 94.3 jit_solution(17972896571422641278)
XLA Ops:
  0.6 0.0 copy-start
  0.6 0.0 copy-start.1
  0.7 0.0 copy-start.4
  0.7 52.5 %tangent.1 = (f32[18,34,8,128]{3,2,1,0:T(8,128)}, f32[18,34,8,128]{3,2,1,0:T(8,128)}, s32[64,128]{1,0:T(8,128)}, f32[16,128]{1,0:T(8,128)}) custom-call(s32[64,128]{1,0:T(8,128)} %cells_v.1, s32[64]{0:T(128)} %plane_s.1, f32[64,64,128]{2,1,0:T(8,128)} %bitcast.20, f32[64,64,128]{2,1,0:T(8,128)} %bitcast.21, f32[64,64,128]{2,1,0:T(8,128)} %bitcast.22, ...), custom_call_target="tpu_custom_call" | custom-call | tf_op jit(solution)/shard_map/tangent/pallas_call | solution.py:570
  53.2 0.0 copy-done
  53.2 0.0 copy-done.1
  53.2 0.0 copy-done.4
  53.2 0.0 copy-start.2
  53.2 0.7 copy-done.2
  54.0 0.0 copy-start.3
  54.0 0.7 copy-done.3
  54.7 14.0 %scatter.1 = (f32[4096,128]{1,0:T(8,128)S(1)}, f32[32,40]{1,0:T(8,128)}) custom-call(s32[64,128]{1,0:T(8,128)S(1)} %copy-done.2, s32[64]{0:T(128)S(1)} %copy-done.4, s32[64,128]{1,0:T(8,128)S(1)} %copy-done.1, bf16[64,32,128]{2,1,0:T(8,128)(2,1)S(1)} %copy-done, f32[16,128]{1,0:T(8,128)S(1)} %copy-done.3), custom_call_target="tpu_custom_call" | custom-call | tf_op jit(solution)/shard_map/scatter/pallas_call | solution.py:589
  68.7 24.1 %adjoint.1 = f32[16,32,8,128]{3,2,1,0:T(8,128)S(1)} custom-call(f32[16,32,8,128]{3,2,1,0:T(8,128)S(1)} %bitcast.19, f32[18,34,8,128]{3,2,1,0:T(8,128)} %get-tuple-element.11.mu_in, f32[18,34,8,128]{3,2,1,0:T(8,128)} %get-tuple-element.12.v_in), custom_call_target="tpu_custom_call" | custom-call | tf_op jit(solution)/shard_map/adjoint/pallas_call | solution.py:599
  92.8 1.5 %reshape.35 = f32[16,32,1024]{2,1,0:T(8,128)} reshape(f32[16,32,8,128]{3,2,1,0:T(8,128)S(1)} %adjoint.1) | data formatting | bytes 4194304 | tf_op jit(solution)/shard_map/reshape | solution.py:609
Async XLA Ops:
  0.6 52.6 %copy-start = (bf16[64,32,128]{2,1,0:T(8,128)(2,1)S(1)}, bf16[64,32,128]{2,1,0:T(8,128)(2,1)}, u32[]{:S(2)}) copy-start(bf16[64,32,128]{2,1,0:T(8,128)(2,1)} %weights.1) | copy-start | bytes 1572868
  0.6 52.6 %copy-start.1 = (s32[64,128]{1,0:T(8,128)S(1)}, s32[64,128]{1,0:T(8,128)}, u32[]{:S(2)}) copy-start(s32[64,128]{1,0:T(8,128)} %cells_v.1) | copy-start | bytes 98308
  0.7 52.6 %copy-start.4 = (s32[64]{0:T(128)S(1)}, s32[64]{0:T(128)}, u32[]{:S(2)}) copy-start(s32[64]{0:T(128)} %plane_s.1) | copy-start | bytes 772
  53.2 0.8 copy-start.2
  54.0 0.7 copy-start.3

commit v4 on v3

--- a/solution.py
+++ b/solution.py
@@ -240,7 +240,7 @@
 
 
 def tangent_kernel(
-    CZ, CY, c_in, p_in, v_in, y_in, s_in, w_in, mu_out, v_out, rows_out, table,
+    CZ, CY, c_in, p_in, v_in, y_in, s_in, w_in, mu_out, v_out, table,
     rows_s, plane_s, cells_v, rows_v, vin, yin, sin, weights, V, MU, DMU, A, R, W1, W2, W3, T, rows0, rows1, held, parts,
     load, store, send, recv, sum_send, sum_recv,
 ):
@@ -284,32 +284,29 @@
             MU[z + 1, y + 1 + s] = 1.0 + yin[i, pl.ds(s, 8, stride=8), :] * reg[s]
             DMU[z + 1, y + 1 + s] = sin[i, pl.ds(s, 8, stride=8), :] * reg[s]
 
-    @pl.loop(0, CZ - 1)
-    def _(z):
-        for t in range(tiles - 1):
-            viscosity(z, t)
+    some = divisor(CZ - 1, 3)
+
+    @pl.loop(0, (CZ - 1) // some)
+    def _(i):
+        for j in range(some):
+            for t in range(tiles - 1):
+                viscosity(i * some + j, t)
 
     faces.arrive(V, 0)
     for t in range(tiles):
         viscosity(CZ - 1, t)
 
-    pair = divisor(CZ - 1, 3)
-
-    @pl.loop(0, (CZ - 1) // pair)
+    @pl.loop(0, (CZ - 1) // some)
     def _(i):
-        for j in range(pair):
-            viscosity(i * pair + j, tiles - 1)
+        for j in range(some):
+            viscosity(i * some + j, tiles - 1)
 
     faces.start(MU, 1)
     faces.start(DMU, 2)
     loads[4].wait()
     rows_v[...] = cells_v[...] >> 7
-    numbers = [
-        pltpu.make_async_copy(rows_v, dst, store.at[2 + i])
-        for i, dst in enumerate((rows_s, rows_out))
-    ]
-    for c in numbers:
-        c.start()
+    numbers = pltpu.make_async_copy(rows_v, rows_s, store.at[2])
+    numbers.start()
 
     def source(z, y, zn, yn):
         zs, ys = pl.ds(z, zn), pl.ds(y, yn)
@@ -327,7 +324,7 @@
         R[zs, ys] = first
         W1[pl.ds(z + 1, zn), pl.ds(y + 1, yn)] = first
 
-    interior(CZ, CY, source, 1)
+    interior(CZ, CY, source, 2)
     faces.arrive(MU, 1)
     faces.arrive(DMU, 2)
     stores = [
@@ -346,12 +343,12 @@
 
     loads[3].wait()
     loads[5].wait()
-    numbers[0].wait()
+    numbers.wait()
     observe(rows_s, plane_s, cells_v, weights, T, parts, (rows0, rows1))
     sum_all(parts, table, held, sum_send, sum_recv)
     for e, buf in enumerate((V, MU, DMU, W1, W2, W3)):
         faces.finish(buf, e)
-    for c in stores + numbers[1:]:
+    for c in stores:
         c.wait()
 
 
@@ -393,14 +390,14 @@
         T[zs, ys] = (-0.5 * regularized(dz, dy, dx)) * total
 
     boundary(CZ, CY, begin, functools.partial(faces.leave, W1, 0))
-    interior(CZ, CY, begin, 1)
+    interior(CZ, CY, begin, 2)
     for step, (src, dst) in enumerate(((W1, W2), (W2, W3), (W3, W4))):
         go = functools.partial(sweep, A, R, src, put_padded(dst))
         interior(CZ, CY, go, 2)
         faces.arrive(src, step)
         boundary(CZ, CY, go, functools.partial(faces.leave, dst, step + 1))
     loads[2].wait()
-    interior(CZ, CY, product, 1)
+    interior(CZ, CY, product, 2)
     faces.arrive(W4, 3)
     boundary(CZ, CY, product)
     last = pltpu.make_async_copy(T, out, store)
@@ -485,8 +482,14 @@
         c.wait_send()
 
 
-def scatter_kernel(copies, rows_s, plane_s, cells_v, weights, table, out, obs, values0, values1, *accs):
+def scatter_kernel(
+    copies, plane_s, cells_v, weights, table, out, obs,
+    rows_s, rows_v, values0, values1, sem, *accs,
+):
     B, K = rows_s.shape
+    rows_v[...] = cells_v[...] >> 7
+    numbers = pltpu.make_async_copy(rows_v, rows_s, sem)
+    numbers.start()
     group = values0.shape[0] // K
     size = out.shape[0]
     accs3 = [by_row(acc) for acc in accs]
@@ -525,6 +528,7 @@
                     accs3[i][at[i]] = new[i]
 
     spread(0, values0)
+    numbers.wait()
 
     @pl.loop(0, B // (2 * group))
     def _(i):
@@ -565,19 +569,18 @@
         )
 
     DMA = pltpu.SemaphoreType.DMA
-    numbers = jax.ShapeDtypeStruct((B, K), jnp.int32)
-    held, spare = [vm((divisor(B // 2, 4) * K, 128))] * 2, [vm((divisor(B // 2, 2) * K, 128))] * 2
-    mu, vel, rows, table = pl.pallas_call(
+    held = [vm((divisor(B // 2, 4) * K, 128))] * 2
+    mu, vel, table = pl.pallas_call(
         functools.partial(tangent_kernel, CZ, CY),
-        out_shape=(sds(padded), sds(padded), numbers, sds((16, 128))),
+        out_shape=(sds(padded), sds(padded), sds((16, 128))),
         in_specs=[HBM] * 6,
-        out_specs=(ANY, ANY, ANY, VMEM),
+        out_specs=(ANY, ANY, VMEM),
         scratch_shapes=[pltpu.SMEM((B, K), jnp.int32), pltpu.SMEM((B,), jnp.int32)]
         + [pltpu.VMEM((B, K), jnp.int32)] * 2 + [vm(tiles)] * 3 + [pltpu.VMEM((B, S, K), BF16)]
         + [vm(padded)] * 3 + [vm((6,) + core), vm(core)] + [vm(padded)] * 3
         + [vm((CZ * CY * 8, 128))] + held
         + [vm((3, 8, 16, 128)), vm((3, 16, 128))]
-        + [DMA((6,)), DMA((4,)), DMA((6, 4)), DMA((6, 4)), DMA((3, 8)), DMA((3, 8))],
+        + [DMA((6,)), DMA((3,)), DMA((6, 4)), DMA((6, 4)), DMA((3, 8)), DMA((3, 8))],
         compiler_params=params(56, 0),
         name="tangent",
     )(
@@ -589,12 +592,13 @@
     adj, obs = pl.pallas_call(
         functools.partial(scatter_kernel, copies),
         out_shape=(sds((CZ * CY * 8, 128)), sds((S, PLANES))),
-        in_specs=[SMEM, SMEM, VMEM, VMEM, VMEM],
+        in_specs=[SMEM, VMEM, VMEM, VMEM],
         out_specs=(VMEM, VMEM),
-        scratch_shapes=spare + [vm((CZ * CY * 8, 128))] * copies,
+        scratch_shapes=[pltpu.SMEM((B, K), jnp.int32), pltpu.VMEM((B, K), jnp.int32)]
+        + [vm((K, 128))] * 2 + [DMA] + [vm((CZ * CY * 8, 128))] * copies,
         compiler_params=params(24),
         name="scatter",
-    )(rows, block_plane, block_cells, block_weights, table)
+    )(block_plane, block_cells, block_weights, table)
 
     product = pl.pallas_call(
         functools.partial(adjoint_kernel, CZ, CY),

time: 94.5 us -> 92 us (0.974)
  Pallas kernels: 90.6 us -> 89 us
    pallas_call x1, Pallas kernels: 14 us -> 12.3 us  [shards(): pl.pallas_call(functools.partial(scatter_kernel, copies), out_shape=(sds(...]
where the time goes in v4:
time: 92 us; the launch traced here: 91.9 us
  Pallas kernels  89 us (97%)
  local copies, waits for them, and re-layouts  2.19 us (2%)
    pallas_call x1, Pallas kernels, shards(): pl.pallas_call(functools.partial(tangent_kernel, CZ, CY), out_shape=(sds(...  52.5 us
    pallas_call x1, Pallas kernels, shards(): pl.pallas_call(functools.partial(adjoint_kernel, CZ, CY), out_shape=sds(c...  24.1 us
    pallas_call x1, Pallas kernels, shards(): pl.pallas_call(functools.partial(scatter_kernel, copies), out_shape=(sds(...  12.3 us

profile of v4, /device:TPU:32, one launch (start us, length us, event | category | flops | bytes accessed | tf_op | source)
XLA Modules:
  0.0 91.9 jit_solution(15721325604000367779)
XLA Ops:
  0.6 0.0 copy-start
  0.6 0.0 copy-start.1
  0.7 0.0 copy-start.3
  0.7 52.5 %tangent.1 = (f32[18,34,8,128]{3,2,1,0:T(8,128)}, f32[18,34,8,128]{3,2,1,0:T(8,128)}, f32[16,128]{1,0:T(8,128)}) custom-call(s32[64,128]{1,0:T(8,128)} %cells_v.1, s32[64]{0:T(128)} %plane_s.1, f32[64,64,128]{2,1,0:T(8,128)} %bitcast.20, f32[64,64,128]{2,1,0:T(8,128)} %bitcast.21, f32[64,64,128]{2,1,0:T(8,128)} %bitcast.22, bf16[64,32,128]{2,1,0:T(8,128)(2,1)} %weights.1), custom_call_target="tpu_custom_call" | custom-call | tf_op jit(solution)/shard_map/tangent/pallas_call | solution.py:573
  53.2 0.0 copy-done
  53.2 0.0 copy-done.1
  53.2 0.0 copy-done.3
  53.2 0.0 copy-start.2
  53.2 0.7 copy-done.2
  53.9 12.3 %scatter.1 = (f32[4096,128]{1,0:T(8,128)S(1)}, f32[32,40]{1,0:T(8,128)}) custom-call(s32[64]{0:T(128)S(1)} %copy-done.3, s32[64,128]{1,0:T(8,128)S(1)} %copy-done.1, bf16[64,32,128]{2,1,0:T(8,128)(2,1)S(1)} %copy-done, f32[16,128]{1,0:T(8,128)S(1)} %copy-done.2), custom_call_target="tpu_custom_call" | custom-call | tf_op jit(solution)/shard_map/scatter/pallas_call | solution.py:592
  66.2 24.1 %adjoint.1 = f32[16,32,8,128]{3,2,1,0:T(8,128)S(1)} custom-call(f32[16,32,8,128]{3,2,1,0:T(8,128)S(1)} %bitcast.19, f32[18,34,8,128]{3,2,1,0:T(8,128)} %get-tuple-element.9.mu_in, f32[18,34,8,128]{3,2,1,0:T(8,128)} %get-tuple-element.10.v_in), custom_call_target="tpu_custom_call" | custom-call | tf_op jit(solution)/shard_map/adjoint/pallas_call | solution.py:603
  90.4 1.5 %reshape.35 = f32[16,32,1024]{2,1,0:T(8,128)} reshape(f32[16,32,8,128]{3,2,1,0:T(8,128)S(1)} %adjoint.1) | data formatting | bytes 4194304 | tf_op jit(solution)/shard_map/reshape | solution.py:613
Async XLA Ops:
  0.6 52.6 %copy-start = (bf16[64,32,128]{2,1,0:T(8,128)(2,1)S(1)}, bf16[64,32,128]{2,1,0:T(8,128)(2,1)}, u32[]{:S(2)}) copy-start(bf16[64,32,128]{2,1,0:T(8,128)(2,1)} %weights.1) | copy-start | bytes 1572868
  0.6 52.6 %copy-start.1 = (s32[64,128]{1,0:T(8,128)S(1)}, s32[64,128]{1,0:T(8,128)}, u32[]{:S(2)}) copy-start(s32[64,128]{1,0:T(8,128)} %cells_v.1) | copy-start | bytes 98308
  0.7 52.6 %copy-start.3 = (s32[64]{0:T(128)S(1)}, s32[64]{0:T(128)}, u32[]{:S(2)}) copy-start(s32[64]{0:T(128)} %plane_s.1) | copy-start | bytes 772
  53.2 0.7 copy-start.2

commit v5 on v4

--- a/solution.py
+++ b/solution.py
@@ -337,7 +337,7 @@
     for step, (src, dst) in enumerate(((W1, W2), (W2, W3), (W3, None))):
         put = put_rows(T, CY) if dst is None else put_padded(dst)
         go = functools.partial(sweep, A, R, src, put)
-        interior(CZ, CY, go, 2)
+        interior(CZ, CY, go, 7)
         faces.arrive(src, 3 + step)
         boundary(CZ, CY, go, dst is not None and functools.partial(faces.leave, dst, 4 + step))
 
@@ -393,7 +393,7 @@
     interior(CZ, CY, begin, 2)
     for step, (src, dst) in enumerate(((W1, W2), (W2, W3), (W3, W4))):
         go = functools.partial(sweep, A, R, src, put_padded(dst))
-        interior(CZ, CY, go, 2)
+        interior(CZ, CY, go, 7)
         faces.arrive(src, step)
         boundary(CZ, CY, go, functools.partial(faces.leave, dst, step + 1))
     loads[2].wait()

time: 92 us -> 92 us (level)
  no operation moved by 1% of the time
where the time goes in v5:
time: 92 us; the launch traced here: 91.9 us
  Pallas kernels  89 us (97%)
  local copies, waits for them, and re-layouts  2.19 us (2%)
    pallas_call x1, Pallas kernels, shards(): pl.pallas_call(functools.partial(tangent_kernel, CZ, CY), out_shape=(sds(...  52.5 us
    pallas_call x1, Pallas kernels, shards(): pl.pallas_call(functools.partial(adjoint_kernel, CZ, CY), out_shape=sds(c...  24.1 us
    pallas_call x1, Pallas kernels, shards(): pl.pallas_call(functools.partial(scatter_kernel, copies), out_shape=(sds(...  12.3 us

profile of v5, /device:TPU:32, one launch (start us, length us, event | category | flops | bytes accessed | tf_op | source)
XLA Modules:
  0.0 91.9 jit_solution(16949746435027392099)
XLA Ops:
  0.6 0.0 copy-start
  0.6 0.0 copy-start.1
  0.7 0.0 copy-start.3
  0.7 52.5 %tangent.1 = (f32[18,34,8,128]{3,2,1,0:T(8,128)}, f32[18,34,8,128]{3,2,1,0:T(8,128)}, f32[16,128]{1,0:T(8,128)}) custom-call(s32[64,128]{1,0:T(8,128)} %cells_v.1, s32[64]{0:T(128)} %plane_s.1, f32[64,64,128]{2,1,0:T(8,128)} %bitcast.20, f32[64,64,128]{2,1,0:T(8,128)} %bitcast.21, f32[64,64,128]{2,1,0:T(8,128)} %bitcast.22, bf16[64,32,128]{2,1,0:T(8,128)(2,1)} %weights.1), custom_call_target="tpu_custom_call" | custom-call | tf_op jit(solution)/shard_map/tangent/pallas_call | solution.py:573
  53.2 0.0 copy-done
  53.2 0.0 copy-done.1
  53.2 0.0 copy-done.3
  53.2 0.0 copy-start.2
  53.3 0.7 copy-done.2
  53.9 12.3 %scatter.1 = (f32[4096,128]{1,0:T(8,128)S(1)}, f32[32,40]{1,0:T(8,128)}) custom-call(s32[64]{0:T(128)S(1)} %copy-done.3, s32[64,128]{1,0:T(8,128)S(1)} %copy-done.1, bf16[64,32,128]{2,1,0:T(8,128)(2,1)S(1)} %copy-done, f32[16,128]{1,0:T(8,128)S(1)} %copy-done.2), custom_call_target="tpu_custom_call" | custom-call | tf_op jit(solution)/shard_map/scatter/pallas_call | solution.py:592
  66.3 24.1 %adjoint.1 = f32[16,32,8,128]{3,2,1,0:T(8,128)S(1)} custom-call(f32[16,32,8,128]{3,2,1,0:T(8,128)S(1)} %bitcast.19, f32[18,34,8,128]{3,2,1,0:T(8,128)} %get-tuple-element.9.mu_in, f32[18,34,8,128]{3,2,1,0:T(8,128)} %get-tuple-element.10.v_in), custom_call_target="tpu_custom_call" | custom-call | tf_op jit(solution)/shard_map/adjoint/pallas_call | solution.py:603
  90.4 1.5 %reshape.35 = f32[16,32,1024]{2,1,0:T(8,128)} reshape(f32[16,32,8,128]{3,2,1,0:T(8,128)S(1)} %adjoint.1) | data formatting | bytes 4194304 | tf_op jit(solution)/shard_map/reshape | solution.py:613
Async XLA Ops:
  0.6 52.6 %copy-start = (bf16[64,32,128]{2,1,0:T(8,128)(2,1)S(1)}, bf16[64,32,128]{2,1,0:T(8,128)(2,1)}, u32[]{:S(2)}) copy-start(bf16[64,32,128]{2,1,0:T(8,128)(2,1)} %weights.1) | copy-start | bytes 1572868
  0.6 52.6 %copy-start.1 = (s32[64,128]{1,0:T(8,128)S(1)}, s32[64,128]{1,0:T(8,128)}, u32[]{:S(2)}) copy-start(s32[64,128]{1,0:T(8,128)} %cells_v.1) | copy-start | bytes 98308
  0.7 52.6 %copy-start.3 = (s32[64]{0:T(128)S(1)}, s32[64]{0:T(128)}, u32[]{:S(2)}) copy-start(s32[64]{0:T(128)} %plane_s.1) | copy-start | bytes 772
  53.2 0.7 copy-start.2
